TPU v7x, 256 devices: a whole 4x4x8 slice. The times are simulated.
256 devices in a mesh: dp: 16 (over x, z_hi), pipe: 2 (over z_lo), tensor: 8 (over y, core).
Axes of the slice: x: 4, y: 4, z: 8 (z_hi: 4, z_lo: 2; z = z_hi * 2 + z_lo), core: 2. Of those that a mesh axis runs over, the one named last changes fastest.
Arguments:
- sent_qkv: bfloat16 [2, 16, 384, 3, 6144], P('pipe', 'dp', None, None, 'tensor'), may hold values from -64 to 64
- saved_qkv: bfloat16 [2, 16, 384, 3, 6144], P('pipe', 'dp', None, None, 'tensor'), may hold values from -64 to 64
- cotangent: bfloat16 [2, 16, 384, 6144], P('pipe', 'dp', None, 'tensor'), may hold values from -6 to 6
- out_weight: bfloat16 [2, 6144, 6144], P('pipe', 'tensor', 'dp'), may hold values from -0.078125 to 0.078125
Outputs:
- section_out: bfloat16 [2, 16, 384, 6144], P('pipe', 'dp', None, 'tensor')
- qkv_grad: bfloat16 [2, 16, 384, 3, 6144], P('pipe', 'dp', None, None, 'tensor')
- weight_grad: bfloat16 [2, 6144, 6144], P('pipe', 'tensor', 'dp')
All inputs are finite; a program needn't handle non-finite values.
Results may differ from a plain program's by a relative error of at most 0.019.
Values may be sent and summed in bfloat16 or wider, within the bound.
A program may use at most 128 MiB of HBM per device.

v0:
```python
import math

import jax
import jax.numpy as jnp
from jax import lax
from jax.sharding import PartitionSpec as P

HEAD_DIM = 128


def passed_along(value, axis, steps):
    count = lax.axis_size(axis)
    pairs = [(source, (source + steps) % count) for source in range(count)]
    return lax.ppermute(value, axis, pairs)


def heads_forward(triple):
    seq_rows = triple.shape[0]
    local_heads = triple.shape[2] // HEAD_DIM
    pieces = triple.reshape(seq_rows, 3, local_heads, HEAD_DIM)
    scores = jnp.einsum(
        "ihd,jhd->hij", pieces[:, 0], pieces[:, 1], preferred_element_type=jnp.float32
    ) / math.sqrt(HEAD_DIM)
    causal = jnp.arange(seq_rows)[:, None] >= jnp.arange(seq_rows)[None, :]
    scores = jnp.where(causal[None], scores, -jnp.inf)
    attention_w = jax.nn.softmax(scores, axis=-1)
    attention_b = attention_w.astype(jnp.bfloat16)
    context = jnp.einsum(
        "hij,jhd->ihd", attention_b, pieces[:, 2], preferred_element_type=jnp.float32
    )
    return (
        attention_w,
        attention_b,
        context.reshape(seq_rows, local_heads * HEAD_DIM).astype(jnp.bfloat16),
    )


def heads_backward(triple, attention_w, attention_b, context_grad):
    seq_rows = triple.shape[0]
    local_heads = triple.shape[2] // HEAD_DIM
    pieces = triple.reshape(seq_rows, 3, local_heads, HEAD_DIM)
    upstream = context_grad.reshape(seq_rows, local_heads, HEAD_DIM)
    attention_dw = jnp.einsum(
        "ihd,jhd->hij", upstream, pieces[:, 2], preferred_element_type=jnp.float32
    )
    row_total = jnp.sum(attention_w * attention_dw, axis=-1, keepdims=True)
    score_grad = (attention_w * (attention_dw - row_total) / math.sqrt(HEAD_DIM)).astype(
        jnp.bfloat16
    )
    query_grad = jnp.einsum(
        "hij,jhd->ihd", score_grad, pieces[:, 1], preferred_element_type=jnp.float32
    )
    key_grad = jnp.einsum(
        "hij,ihd->jhd", score_grad, pieces[:, 0], preferred_element_type=jnp.float32
    )
    value_grad = jnp.einsum(
        "hij,ihd->jhd", attention_b, upstream, preferred_element_type=jnp.float32
    )
    stacked = jnp.stack([query_grad, key_grad, value_grad], axis=1).astype(jnp.bfloat16)
    return stacked.reshape(seq_rows, 3, local_heads * HEAD_DIM)


def forward_pass(sent_qkv, weight):
    received = passed_along(sent_qkv, "pipe", 1)
    forward_w, forward_b, context_a = heads_forward(received[0, 0])
    section_cols = lax.psum_scatter(
        lax.dot_general(
            weight, context_a, (((0,), (1,)), ((), ())), preferred_element_type=jnp.float32
        ).astype(jnp.bfloat16),
        "tensor",
        scatter_dimension=0,
        tiled=True,
    ).astype(jnp.float32)
    return section_cols.T.astype(jnp.bfloat16)[None, None]


def backward_pass(saved_qkv, cotangent, weight):
    upstream = lax.all_gather(cotangent, "tensor", axis=3, tiled=True)[0, 0]
    triple = saved_qkv[0, 0]
    backward_w, backward_b, context_b = heads_forward(triple)
    summed = lax.psum_scatter(
        lax.dot_general(
            upstream, context_b, (((0,), (0,)), ((), ())), preferred_element_type=jnp.float32
        ).astype(jnp.bfloat16),
        "dp",
        scatter_dimension=0,
        tiled=True,
    ).astype(jnp.float32)
    weight_grad = (summed.T / lax.axis_size("dp")).astype(jnp.bfloat16)[None]
    context_grad = lax.dot_general(
        upstream, weight, (((1,), (1,)), ((), ())), preferred_element_type=jnp.float32
    )
    triple_grad = heads_backward(triple, backward_w, backward_b, context_grad.astype(jnp.bfloat16))
    return (triple_grad[None, None], weight_grad)


def body(sent_qkv, saved_qkv, cotangent, out_weight):
    weight = lax.all_gather(out_weight, "dp", axis=2, tiled=True)[0]
    section_out = forward_pass(sent_qkv, weight)
    triple_grad, weight_grad = backward_pass(saved_qkv, cotangent, weight)
    return (section_out, triple_grad, weight_grad)


def solution(mesh):
    in_specs = (
        P("pipe", "dp", None, None, "tensor"),
        P("pipe", "dp", None, None, "tensor"),
        P("pipe", "dp", None, "tensor"),
        P("pipe", "tensor", "dp"),
    )
    out_specs = (
        P("pipe", "dp", None, "tensor"),
        P("pipe", "dp", None, None, "tensor"),
        P("pipe", "tensor", "dp"),
    )
    return jax.shard_map(body, mesh=mesh, in_specs=in_specs, out_specs=out_specs, check_vma=False)
```

profile of v0, /device:TPU:1, one launch (start us, length us, event | category | flops | bytes accessed | tf_op | source)
XLA Modules:
  0.0 396.1 jit_solution(17203349348232318335)
XLA Ops:
  7.2 0.0 all-gather.5.cloned.1.call-start
  7.2 0.7 all-gather.5.cloned.1.call-update
  7.9 0.0 all-gather.3.cloned.1.call-start
  7.9 0.7 all-gather.3.cloned.1.call-update
  8.6 0.0 reduce-scatter.7.cloned.1.call-start
  8.7 2.8 copy.45
  11.5 0.0 copy-start.1
  11.5 0.7 fusion.52
  12.2 1.2 fusion.63
  13.4 0.0 copy-done.1
  13.4 0.0 copy-start.3
  13.4 1.8 copy-done.3
  15.2 0.6 convolution_convert_fusion.1
  15.8 35.2 %all-gather.5.cloned.1.call-done = bf16[1,1,384,6144]{3,2,1,0:T(8,128)(2,1)} async-done(((bf16[1,1,384,768]{3,2,1,0:T(8,128)(2,1)}), bf16[1,1,384,6144]{3,2,1,0:T(8,128)(2,1)}) %all-gather.5.cloned.1.call-update) | async-done | bytes 4718608 | tf_op jit(solution)/shard_map/all_gather | solution.py:78
  51.0 9.8 %fusion.7 = bf16[6144,768]{0,1:T(8,128)(2,1)} fusion(bf16[384,768]{0,1:T(8,128)(2,1)S(1)} %bitcast.95, bf16[1,1,384,6144]{3,2,1,0:T(8,128)(2,1)} %all-gather.5.cloned.1.call-done), kind=kOutput, calls=%fused_computation.8 | convolution fusion | flops 3628597248 | bytes 14745600 | tf_op jit(solution)/shard_map/dot_general | solution.py:82
  60.8 12.8 %copy.70 = bf16[6144,768]{1,0:T(8,128)(2,1)} copy(bf16[6144,768]{0,1:T(8,128)(2,1)} %fusion.7) | data formatting | bytes 18874368
  73.6 0.0 copy-start
  73.6 0.0 reduce-scatter.7.cloned.1.call-update
  73.6 0.0 reduce-scatter.5.cloned.1.call-start
  73.6 1.4 copy-done
  75.1 2.2 copy.41
  77.3 0.0 copy-start.2
  77.3 1.3 collective-permute-start
  78.5 98.3 %collective-permute-done = bf16[1,1,384,3,768]{2,4,3,1,0:T(8,128)(2,1)S(1)} collective-permute-done((bf16[1,1,384,3,768]{2,4,3,1,0:T(8,128)(2,1)}, bf16[1,1,384,3,768]{2,4,3,1,0:T(8,128)(2,1)S(1)}, u32[]{:S(2)}, u32[]{:S(2)}) %collective-permute-start) | collective-permute-done | bytes 1769504 | tf_op jit(solution)/shard_map/ppermute | solution.py:14
  176.8 0.7 fusion.51
  177.5 0.0 copy-done.2
  177.5 1.2 fusion.62
  178.7 0.6 fusion.36
  179.3 37.1 %all-gather.3.cloned.1.call-done = bf16[1,768,6144]{2,1,0:T(8,128)(2,1)} async-done(((bf16[1,768,384]{2,1,0:T(8,128)(2,1)}), bf16[1,768,6144]{2,1,0:T(8,128)(2,1)}) %all-gather.3.cloned.1.call-update) | async-done | bytes 9437200 | tf_op jit(solution)/shard_map/all_gather | solution.py:98
  216.4 9.3 %fusion.11 = bf16[6144,384]{0,1:T(8,128)(2,1)} fusion(bf16[384,768]{0,1:T(8,128)(2,1)S(1)} %bitcast.90, bf16[1,768,6144]{2,1,0:T(8,128)(2,1)} %all-gather.3.cloned.1.call-done), kind=kOutput, calls=%fused_computation.10 | convolution fusion | flops 3626237952 | bytes 14745600 | tf_op jit(solution)/shard_map/dot_general | solution.py:67
  225.6 0.0 reduce-scatter.5.cloned.1.call-update
  225.7 9.1 %fusion.43 = bf16[384,768]{1,0:T(8,128)(2,1)S(1)} fusion(bf16[1,768,6144]{2,1,0:T(8,128)(2,1)} %all-gather.3.cloned.1.call-done, bf16[1,1,384,6144]{3,2,1,0:T(8,128)(2,1)} %all-gather.5.cloned.1.call-done), kind=kOutput, calls=%fused_computation.39 | convolution fusion | flops 3624173568 | bytes 14745600 | tf_op jit(solution)/shard_map/dot_general | solution.py:90
  234.7 0.3 copy.48
  235.0 2.7 convolution_convert_fusion.2
  237.8 0.3 copy.58
  238.0 2.4 fusion.53
  240.5 6.4 %fusion.40 = bf16[6,384,128]{1,2,0:T(8,128)(2,1)S(1)} fusion(f32[6,384,384]{1,2,0:T(8,128)} %fusion.53, bf16[384,3,6,128]{0,3,2,1:T(8,128)(2,1)S(1)} %bitcast.84, f32[6,384,384]{1,2,0:T(8,128)} %copy-done.3, f32[6,384]{1,0:T(8,128)S(1)} %get-tuple-element.5), kind=kOutput, calls=%fused_computation.38 | convolution fusion | flops 232983168 | bytes 15360000 | tf_op jit(solution)/shard_map/hij,ihd->jhd/dot_general | solution.py:53
  246.8 0.3 copy.57
  247.1 6.4 %fusion.37 = bf16[6,384,128]{1,2,0:T(8,128)(2,1)S(1)} fusion(f32[6,384,384]{1,2,0:T(8,128)} %fusion.53, bf16[384,3,6,128]{0,3,2,1:T(8,128)(2,1)S(1)} %bitcast.85, f32[6,384,384]{1,2,0:T(8,128)} %copy-done.3, f32[6,384]{1,0:T(8,128)S(1)} %get-tuple-element.5), kind=kOutput, calls=%fused_computation.37 | convolution fusion | flops 232983168 | bytes 15360000 | tf_op jit(solution)/shard_map/hij,jhd->ihd/dot_general | solution.py:50
  253.5 0.3 copy.56
  253.8 1.4 pad_maximum_fusion
  255.2 93.7 %reduce-scatter.7.cloned.1.call-done = bf16[384,768]{1,0:T(8,128)(2,1)} async-done(((bf16[6144,768]{1,0:T(8,128)(2,1)}), bf16[384,768]{1,0:T(8,128)(2,1)}) %reduce-scatter.7.cloned.1.call-update) | async-done | bytes 589840
  348.8 1.4 copy.71
  350.2 0.9 fusion.50
  351.1 38.5 %reduce-scatter.5.cloned.1.call-done = bf16[768,384]{0,1:T(8,128)(2,1)} async-done(((bf16[6144,384]{0,1:T(8,128)(2,1)}), bf16[768,384]{0,1:T(8,128)(2,1)}) %reduce-scatter.5.cloned.1.call-update) | async-done | bytes 589840 | tf_op jit(solution)/shard_map/reduce_scatter | solution.py:66
  (1 shorter events, 0.0 us)
Async XLA Ops:
  7.2 43.8 %all-gather.5.cloned.1.call-start = ((), (), s32[]{:S(2)}) async-start(), calls=%async_computation.4 | async-start | bytes 5308416 | tf_op jit(solution)/shard_map/all_gather | solution.py:78
  7.9 208.5 %all-gather.3.cloned.1.call-start = ((), (), s32[]{:S(2)}) async-start(), calls=%async_computation.2 | async-start | bytes 10027008 | tf_op jit(solution)/shard_map/all_gather | solution.py:98
  8.6 340.2 %reduce-scatter.7.cloned.1.call-start = ((), (), s32[]{:S(2)}) async-start(), calls=%async_computation.5 | async-start | bytes 10027008
  11.5 1.9 copy-start.1
  13.4 1.8 copy-start.3
  73.6 1.5 copy-start
  73.6 316.0 %reduce-scatter.5.cloned.1.call-start = ((), (), s32[]{:S(2)}) async-start(), calls=%async_computation.3 | async-start | bytes 5308416 | tf_op jit(solution)/shard_map/reduce_scatter | solution.py:66
  77.3 100.2 %copy-start.2 = (pred[384,384]{0,1:T(8,128)(4,1)S(1)}, pred[384,384]{0,1:T(8,128)(4,1)}, u32[]{:S(2)}) copy-start(pred[384,384]{0,1:T(8,128)(4,1)} %copy-done.1) | copy-start | bytes 442372
  77.3 99.5 %collective-permute-start = (bf16[1,1,384,3,768]{2,4,3,1,0:T(8,128)(2,1)}, bf16[1,1,384,3,768]{2,4,3,1,0:T(8,128)(2,1)S(1)}, u32[]{:S(2)}, u32[]{:S(2)}) collective-permute-start(bf16[1,1,384,3,768]{2,4,3,1,0:T(8,128)(2,1)} %copy.41), channel_id=1, source_target_pairs={{0,8},{8,0},{1,9},{9,1},{2,10},{10,2},{3,11},{11,3},{4,12},{12,4},... | collective-permute-start | bytes 5308424 | tf_op jit(solution)/shard_map/ppermute | solution.py:14
Sparse Core Ops, SparseCore 0:
  9.8 41.0 all-gather.4
  53.4 162.9 all-gather.2
  220.1 128.6 reduce-scatter.6
  352.0 37.5 reduce-scatter.4
where the time goes:
time: 399 us; the launch traced here: 396 us
  waiting for transfers between devices  304 us (76%)
  matrix products  48.6 us (12%)
  local copies, waits for them, and re-layouts  23.4 us (6%)
  between operations  13.9 us (3%)
  other arithmetic  4.79 us (1%)
    ppermute x1, waiting for transfers between devices, passed_along(): return lax.ppermute(value, axis, pairs)  98.3 us
    unnamed x5, waiting for transfers between devices  95.1 us
    reduce_scatter x1, waiting for transfers between devices, forward_pass(): lax.psum_scatter(lax.dot_general(weight, context_a, (((0,), (1,)), ((), (...  38.5 us
    all_gather x1, waiting for transfers between devices, body(): weight = lax.all_gather(out_weight, 'dp', axis=2, tiled=True)[0]  37.1 us
    all_gather x1, waiting for transfers between devices, backward_pass(): upstream = lax.all_gather(cotangent, 'tensor', axis=3, tiled=True)[0, 0]  35.2 us
    unnamed x12, local copies, waits for them, and re-layouts  22.3 us
    dot_general x1, matrix products, backward_pass(): lax.dot_general(upstream, context_b, (((0,), (0,)), ((), ())), preferred_...  9.81 us
    dot_general x1, matrix products, forward_pass(): lax.dot_general(weight, context_a, (((0,), (1,)), ((), ())), preferred_el...  9.27 us
  transfers between devices with their start and end apart: 5, of which 5 were waited for; matrix products, arithmetic and copies ran while one was open for 19% of the time, Pallas kernels for 0%

commit v1 on v0

v1 whole, which is shorter than its diff:
```python
import math

import jax
import jax.numpy as jnp
from jax import lax
from jax.experimental import pallas as pl
from jax.experimental.pallas import tpu as pltpu
from jax.sharding import PartitionSpec as P

HEAD_DIM = 128
SCALE = 1.0 / math.sqrt(HEAD_DIM)
MESH = pl.DeviceIdType.MESH
BF = jnp.bfloat16
F32 = jnp.float32
S = 384
W = 768
HEADS = W // HEAD_DIM
N_SEMS = 64

NT = (((1,), (1,)), ((), ()))
TN = (((0,), (0,)), ((), ()))


def at(index, size):
    return pl.ds(pl.multiple_of(index * size, size), size)


def mod4(i):
    return lax.rem(i + 4, 4)


def attend(qkv, h):
    cols = at(h, HEAD_DIM)
    scores = lax.dot_general(qkv[0, :, cols], qkv[1, :, cols], NT, preferred_element_type=F32)
    row = lax.broadcasted_iota(jnp.int32, (S, S), 0)
    col = lax.broadcasted_iota(jnp.int32, (S, S), 1)
    scores = jnp.where(row >= col, scores * SCALE, -jnp.inf)
    weights = jnp.exp(scores - jnp.max(scores, axis=1, keepdims=True))
    probs = weights / jnp.sum(weights, axis=1, keepdims=True)
    return jnp.dot(probs.astype(BF), qkv[2, :, cols], preferred_element_type=F32).astype(BF)


def attend_t(qkv, h, probs_t):
    cols = at(h, HEAD_DIM)
    scores = lax.dot_general(qkv[1, :, cols], qkv[0, :, cols], NT, preferred_element_type=F32)
    row = lax.broadcasted_iota(jnp.int32, (S, S), 0)
    col = lax.broadcasted_iota(jnp.int32, (S, S), 1)
    scores = jnp.where(row <= col, scores * SCALE, -jnp.inf)
    weights = jnp.exp(scores - jnp.max(scores, axis=0, keepdims=True))
    probs = weights / jnp.sum(weights, axis=0, keepdims=True)
    probs_t[h] = probs
    return lax.dot_general(
        qkv[2, :, cols], probs.astype(BF), TN, preferred_element_type=F32
    ).astype(BF)


def attend_grad(qkv, h, probs_t, upstream, grads):
    cols = at(h, HEAD_DIM)
    probs = probs_t[h]
    up = upstream[:, cols]
    d_probs = lax.dot_general(qkv[2, :, cols], up, NT, preferred_element_type=F32)
    total = jnp.sum(probs * d_probs, axis=0, keepdims=True)
    d_scores = (probs * (d_probs - total) * SCALE).astype(BF)
    dq_t = lax.dot_general(qkv[1, :, cols], d_scores, TN, preferred_element_type=F32)
    grads[0, :, cols] = dq_t.T.astype(BF)
    grads[1, :, cols] = jnp.dot(d_scores, qkv[0, :, cols], preferred_element_type=F32).astype(BF)
    grads[2, :, cols] = jnp.dot(probs.astype(BF), up, preferred_element_type=F32).astype(BF)


class Ring:
    def __init__(self, remote, me, plus, minus):
        self.remote, self.me, self.plus, self.minus = remote, me, plus, minus

    def gather_half(self, block, h, source=None):
        src = block(self.me, h) if source is None else source
        dst = block(self.me, h)
        to_plus = self.remote(src, dst, self.plus)
        to_minus = self.remote(src, dst, self.minus)
        first, second = (to_plus, to_minus) if h == 0 else (to_minus, to_plus)
        first.start()
        second.start()
        if h == 0:
            self.plus0, self.minus0 = to_plus, to_minus
        else:
            self.plus1, self.minus1 = to_plus, to_minus

    def gather_forward(self, block):
        prev, nxt = mod4(self.me - 1), mod4(self.me + 1)
        self.plus0.wait_recv()
        self.far0 = self.remote(block(prev, 0), block(prev, 0), self.plus)
        self.far0.start()
        self.minus1.wait_recv()
        self.far1 = self.remote(block(nxt, 1), block(nxt, 1), self.minus)
        self.far1.start()

    def gather_near(self):
        self.plus1.wait_recv()
        self.minus0.wait_recv()

    def gather_far(self):
        self.far0.wait_recv()
        self.far1.wait_recv()

    def reduce_far(self, part, got_far):
        far = mod4(self.me + 2)
        self.r0 = self.remote(part(far, 0), got_far.at[0], self.plus)
        self.r1 = self.remote(part(far, 1), got_far.at[1], self.minus)
        self.r0.start()
        self.r1.start()

    def reduce_near(self, part, got_near):
        nxt, prev = mod4(self.me + 1), mod4(self.me - 1)
        self.r2 = self.remote(part(nxt, 1), got_near.at[0, 1], self.plus)
        self.r3 = self.remote(part(prev, 0), got_near.at[1, 0], self.minus)
        self.r2.start()
        self.r3.start()

    def reduce_pass(self, part, got_far, got_near):
        nxt, prev = mod4(self.me + 1), mod4(self.me - 1)
        self.r0.wait_recv()
        ref = part(nxt, 0)
        ref[...] = (ref[...].astype(F32) + got_far[0].astype(F32)).astype(BF)
        self.r4 = self.remote(ref, got_near.at[0, 0], self.plus)
        self.r4.start()
        self.r1.wait_recv()
        ref = part(prev, 1)
        ref[...] = (ref[...].astype(F32) + got_far[1].astype(F32)).astype(BF)
        self.r5 = self.remote(ref, got_near.at[1, 1], self.minus)
        self.r5.start()

    def reduce_sum(self, part, got_near, h):
        for copy in ((self.r4, self.r3), (self.r2, self.r5))[h]:
            copy.wait_recv()
        total = part(self.me, h)[...].astype(F32)
        return total + got_near[0, h].astype(F32) + got_near[1, h].astype(F32)


def kernel(
    qkv_a_hbm, qkv_b_hbm, cot_hbm, w_hbm,
    out_ref, grads_ref, w_grad_ref,
    qkv_a, qkv_b, w_all, cot_all, ctx_a, ctx_a_all, ctx_b_all, probs_t,
    w_part, w_far, w_near, c_part, c_far, c_near, c_grad,
    o_own, o_other, o_got, o_far, o_near, o_done,
    send_sems, recv_sems, local_sems,
):
    dp, pipe, tensor = lax.axis_index("dp"), lax.axis_index("pipe"), lax.axis_index("tensor")
    x, z, y, core = dp // 4, lax.rem(dp, 4), tensor // 2, lax.rem(tensor, 2)

    def device(x=x, z=z, pipe=pipe, y=y, core=core):
        return (x * 4 + z, pipe, y * 2 + core)

    x_plus, x_minus = device(x=mod4(x + 1)), device(x=mod4(x - 1))
    y_plus, y_minus = device(y=mod4(y + 1)), device(y=mod4(y - 1))
    z_plus, z_minus = device(z=mod4(z + 1)), device(z=mod4(z - 1))
    twin, other_pipe, mirror = device(core=1 - core), device(pipe=1 - pipe), device(x=y, y=x)
    off_diagonal = x != y

    barrier = pltpu.get_barrier_semaphore()
    for partner in (x_plus, x_minus, y_plus, y_minus, z_plus, z_minus, twin, other_pipe):
        pl.semaphore_signal(barrier, inc=1, device_id=partner, device_id_type=MESH)

    @pl.when(off_diagonal)
    def _():
        pl.semaphore_signal(barrier, inc=1, device_id=mirror, device_id_type=MESH)

    pl.semaphore_wait(barrier, jnp.where(off_diagonal, 9, 8))

    made = []

    def remote(src, dst, where):
        copy = pltpu.make_async_remote_copy(
            src_ref=src, dst_ref=dst,
            send_sem=send_sems.at[len(made)], recv_sem=recv_sems.at[len(made)],
            device_id=where, device_id_type=MESH,
        )
        made.append(copy)
        return copy

    def w_block(i, h):
        return w_all.at[pl.ds(h * S, S), at(i, S)]

    def cot_block(i, h):
        return cot_all.at[at(2 * i + h, S // 2), at(core, W)]

    def ctx_a_block(i, h):
        return ctx_a_all.at[at(i, S), pl.ds(h * S, S)]

    def ctx_b_block(i, h):
        return ctx_b_all.at[pl.ds(h * S, S), at(i, S)]

    def w_part_block(i, h):
        return w_part.at[i, h]

    def c_part_block(i, h):
        return c_part.at[i, h]

    def o_block(i, h):
        return o_own.at[i, h]

    ring_w = Ring(remote, z, z_plus, z_minus)
    ring_cot = Ring(remote, y, y_plus, y_minus)
    ring_a = Ring(remote, x, x_plus, x_minus)
    ring_b = Ring(remote, x, x_plus, x_minus)
    ring_wg = Ring(remote, z, z_plus, z_minus)
    ring_cg = Ring(remote, x, x_plus, x_minus)
    ring_out = Ring(remote, y, y_plus, y_minus)

    for h in (0, 1):
        ring_w.gather_half(w_block, h, w_hbm.at[pl.ds(h * S, S)])
    cot_mine = cot_all.at[at(y, S), at(core, W)]
    cot_there = cot_all.at[at(x, S), at(core, W)]
    mirrored = remote(cot_hbm, cot_there, mirror)
    cot_local = pltpu.make_async_copy(cot_hbm, cot_mine, local_sems.at[0])

    @pl.when(off_diagonal)
    def _():
        mirrored.start()

    @pl.when(jnp.logical_not(off_diagonal))
    def _():
        cot_local.start()

    load_a = pltpu.make_async_copy(qkv_a_hbm, qkv_a, local_sems.at[1])
    load_b = pltpu.make_async_copy(qkv_b_hbm, qkv_b, local_sems.at[2])
    load_w = pltpu.make_async_copy(w_hbm, w_all.at[:, at(z, S)], local_sems.at[3])
    load_a.start()
    load_b.start()
    load_w.start()

    handed = []
    load_a.wait()
    for h in (0, 1):
        def head_a(i, carry, h=h):
            head = h * (HEADS // 2) + i
            ctx_a[:, at(head, HEAD_DIM)] = attend(qkv_a, head)
            return carry
        lax.fori_loop(0, HEADS // 2, head_a, 0)
        copy = remote(ctx_a.at[:, pl.ds(h * S, S)], ctx_a_block(x, h), other_pipe)
        copy.start()
        handed.append(copy)

    load_b.wait()
    for h in (0, 1):
        def head_b(i, carry, h=h):
            head = h * (HEADS // 2) + i
            ctx_b_all[at(head, HEAD_DIM), at(x, S)] = attend_t(qkv_b, head, probs_t)
            return carry
        lax.fori_loop(0, HEADS // 2, head_b, 0)
        ring_b.gather_half(ctx_b_block, h)

    @pl.when(off_diagonal)
    def _():
        mirrored.wait_recv()

    @pl.when(jnp.logical_not(off_diagonal))
    def _():
        cot_local.wait()

    def to_twin(i):
        ref = cot_all.at[at(i, S), at(core, W)]
        copy = remote(ref, ref, twin)
        copy.start()
        return copy

    for h in (0, 1):
        ring_cot.gather_half(cot_block, h)
    twins = [to_twin(y)]
    ring_b.gather_forward(ctx_b_block)
    for h in (0, 1):
        handed[h].wait_recv()
        ring_a.gather_half(ctx_a_block, h)
    ring_cot.gather_forward(cot_block)
    ring_w.gather_forward(w_block)
    ring_cot.gather_near()
    twins += [to_twin(mod4(y - 1)), to_twin(mod4(y + 1))]
    ring_a.gather_forward(ctx_a_block)
    ring_cot.gather_far()
    twins += [to_twin(mod4(y + 2))]
    ring_b.gather_near()
    ring_b.gather_far()
    for copy in twins:
        copy.wait_recv()

    def w_term(i):
        def rows(r, carry):
            w_part[i, r] = jnp.dot(
                ctx_b_all[at(r, S), :], cot_all[:, at(i, S)], preferred_element_type=F32
            ).astype(BF)
            return carry
        lax.fori_loop(0, 2, rows, 0)

    w_term(mod4(z + 2))
    ring_wg.reduce_far(w_part_block, w_far)
    w_term(mod4(z + 1))
    w_term(mod4(z - 1))
    ring_wg.reduce_near(w_part_block, w_near)
    w_term(z)

    load_w.wait()
    ring_w.gather_near()
    ring_w.gather_far()

    def c_term(i):
        def rows(r, carry):
            c_part[i, r] = lax.dot_general(
                cot_all[at(2 * i + r, S // 2), :], w_all[...], NT, preferred_element_type=F32
            ).astype(BF)
            return carry
        lax.fori_loop(0, 2, rows, 0)

    c_term(mod4(x + 2))
    ring_cg.reduce_far(c_part_block, c_far)
    c_term(mod4(x + 1))
    c_term(mod4(x - 1))
    ring_cg.reduce_near(c_part_block, c_near)
    c_term(x)

    ring_a.gather_near()
    ring_a.gather_far()

    def o_term(i, r, side):
        return jnp.dot(
            ctx_a_all[at(2 * i + r, S // 2), :], w_all[:, at(side, W)], preferred_element_type=F32
        )

    def o_other_rows(j, carry):
        o_other[j // 2, lax.rem(j, 2)] = o_term(j // 2, lax.rem(j, 2), 1 - core).astype(BF)
        return carry

    lax.fori_loop(0, 8, o_other_rows, 0)
    swap = remote(o_other, o_got, twin)
    swap.start()
    ring_wg.reduce_pass(w_part_block, w_far, w_near)
    ring_cg.reduce_pass(c_part_block, c_far, c_near)
    swap.wait_recv()

    def o_sum(i):
        def rows(r, carry):
            o_own[i, r] = (o_term(i, r, core) + o_got[i, r].astype(F32)).astype(BF)
            return carry
        lax.fori_loop(0, 2, rows, 0)

    o_sum(mod4(y + 2))
    ring_out.reduce_far(o_block, o_far)
    o_sum(mod4(y + 1))
    o_sum(mod4(y - 1))
    ring_out.reduce_near(o_block, o_near)
    o_sum(y)

    for h in (0, 1):
        c_grad[pl.ds(h * (S // 2), S // 2)] = ring_cg.reduce_sum(c_part_block, c_near, h).astype(BF)
    ring_out.reduce_pass(o_block, o_far, o_near)

    def head_grad(h, carry):
        attend_grad(qkv_b, h, probs_t, c_grad, grads_ref)
        return carry

    lax.fori_loop(0, HEADS, head_grad, 0)

    for h in (0, 1):
        o_done[pl.ds(h * (S // 2), S // 2)] = ring_out.reduce_sum(o_block, o_near, h).astype(BF)
    back = remote(o_done, out_ref, mirror)

    @pl.when(off_diagonal)
    def _():
        back.start()

    @pl.when(jnp.logical_not(off_diagonal))
    def _():
        out_ref[...] = o_done[...]

    for h in (0, 1):
        w_grad_ref[pl.ds(h * S, S)] = (
            ring_wg.reduce_sum(w_part_block, w_near, h) / lax.axis_size("dp")
        ).astype(BF)

    @pl.when(off_diagonal)
    def _():
        back.wait_recv()

    for copy in made:
        if copy is mirrored or copy is back:
            continue
        copy.wait_send()

    @pl.when(off_diagonal)
    def _():
        mirrored.wait_send()
        back.wait_send()


def body(sent_qkv, saved_qkv, cotangent, out_weight):
    bf = lambda *shape: pltpu.VMEM(shape, BF)
    half = S // 2
    out, grads, w_grad = pl.pallas_call(
        kernel,
        out_shape=(
            jax.ShapeDtypeStruct((S, W), BF),
            jax.ShapeDtypeStruct((3, S, W), BF),
            jax.ShapeDtypeStruct((W, S), BF),
        ),
        in_specs=[pl.BlockSpec(memory_space=pl.ANY)] * 4,
        out_specs=(pl.BlockSpec(memory_space=pltpu.VMEM),) * 3,
        scratch_shapes=[
            bf(3, S, W), bf(3, S, W),
            bf(W, 4 * S), bf(4 * S, 2 * W),
            bf(S, W), bf(4 * S, W), bf(W, 4 * S),
            pltpu.VMEM((HEADS, S, S), F32),
            bf(4, 2, S, S), bf(2, S, S), bf(2, 2, S, S),
            bf(4, 2, half, W), bf(2, half, W), bf(2, 2, half, W), bf(S, W),
            bf(4, 2, half, W), bf(4, 2, half, W), bf(4, 2, half, W),
            bf(2, half, W), bf(2, 2, half, W), bf(S, W),
            pltpu.SemaphoreType.DMA((N_SEMS,)),
            pltpu.SemaphoreType.DMA((N_SEMS,)),
            pltpu.SemaphoreType.DMA((4,)),
        ],
        compiler_params=pltpu.CompilerParams(
            collective_id=0, has_side_effects=True, vmem_limit_bytes=56 << 20
        ),
        cost_estimate=pl.CostEstimate(
            flops=13_000_000_000, bytes_accessed=16_000_000, transcendentals=1_800_000
        ),
    )(
        jnp.transpose(sent_qkv[0, 0], (1, 0, 2)),
        jnp.transpose(saved_qkv[0, 0], (1, 0, 2)),
        cotangent[0, 0],
        out_weight[0],
    )
    return out[None, None], jnp.transpose(grads, (1, 0, 2))[None, None], w_grad[None]


def solution(mesh):
    in_specs = (
        P("pipe", "dp", None, None, "tensor"),
        P("pipe", "dp", None, None, "tensor"),
        P("pipe", "dp", None, "tensor"),
        P("pipe", "tensor", "dp"),
    )
    out_specs = (
        P("pipe", "dp", None, "tensor"),
        P("pipe", "dp", None, None, "tensor"),
        P("pipe", "tensor", "dp"),
    )
    return jax.shard_map(body, mesh=mesh, in_specs=in_specs, out_specs=out_specs, check_vma=False)
```

time: 399 us -> 157 us (0.39)
  the two profiles are of different devices: /device:TPU:1 before, /device:TPU:156 now
where the time goes in v1:
time: 157 us
  Pallas kernels  151 us (96%)
  local copies, waits for them, and re-layouts  5.59 us (4%)
    pallas_call x1, Pallas kernels, body(): pl.pallas_call(kernel, out_shape=(jax.ShapeDtypeStruct((S, W), BF), jax.S...  151 us
    unnamed x5, local copies, waits for them, and re-layouts  5.59 us

profile of v1, /device:TPU:156, one launch (start us, length us, event | category | flops | bytes accessed | tf_op | source)
XLA Modules:
  0.0 156.7 jit_solution(438165359434447472)
XLA Ops:
  0.6 150.5 %shard_map.67 = (bf16[384,768]{1,0:T(8,128)(2,1)}, bf16[3,384,768]{2,1,0:T(8,128)(2,1)}, bf16[768,384]{1,0:T(8,128)(2,1)}) custom-call(bf16[3,384,768]{2,1,0:T(8,128)(2,1)} %bitcast.16, bf16[3,384,768]{2,1,0:T(8,128)(2,1)} %bitcast.17, bf16[384,768]{1,0:T(8,128)(2,1)} %bitcast.18, bf16[768,384]{1,0:T(8,128)(2,1)} %bitcast.19), custom_call_target="tpu_custom_call" | custom-call | flops 12999999488 | bytes 16000000 | tf_op jit(solution)/shard_map/pallas_call | solution.py:395
  151.1 1.9 %copy.10 = bf16[1,1,384,768]{3,2,1,0:T(8,128)(2,1)} copy(bf16[1,1,384,768]{3,2,1,0:T(8,128)(2,1)} %bitcast.15) | data formatting | bytes 1179648
  153.1 0.0 copy-start
  153.1 2.9 %copy.11 = bf16[1,1,384,3,768]{4,2,3,1,0:T(8,128)(2,1)} copy(bf16[1,1,384,3,768]{4,2,3,1,0:T(8,128)(2,1)} %bitcast.13) | data formatting | bytes 3538944
  155.9 0.0 copy-done
  155.9 0.8 copy.12
Async XLA Ops:
  153.1 2.9 %copy-start = (bf16[768,384]{1,0:T(8,128)(2,1)S(1)}, bf16[768,384]{1,0:T(8,128)(2,1)}, u32[]{:S(2)}) copy-start(bf16[768,384]{1,0:T(8,128)(2,1)} %get-tuple-element.8) | copy-start | bytes 1769476

commit v2 on v1

v2 whole, which is shorter than its diff:
```python
import math

import jax
import jax.numpy as jnp
from jax import lax
from jax.experimental import pallas as pl
from jax.experimental.pallas import tpu as pltpu
from jax.sharding import PartitionSpec as P

HEAD_DIM = 128
SCALE = 1.0 / math.sqrt(HEAD_DIM)
MESH = pl.DeviceIdType.MESH
BF = jnp.bfloat16
F32 = jnp.float32
S = 384
W = 768
HEADS = W // HEAD_DIM
N_SEMS = 96
PIECES = S // HEAD_DIM

NT = (((1,), (1,)), ((), ()))
TN = (((0,), (0,)), ((), ()))


def at(index, size):
    return pl.ds(pl.multiple_of(index * size, size), size)


def mod4(i):
    return lax.rem(i + 4, 4)


def causal_blocks():
    for r in range(S // HEAD_DIM):
        yield r, pl.ds(r * HEAD_DIM, HEAD_DIM), pl.ds(0, (r + 1) * HEAD_DIM)


def probs_of_block(qkv, cols, r, mine, seen):
    scores = lax.dot_general(qkv[1, seen, cols], qkv[0, mine, cols], NT, preferred_element_type=F32)
    row = lax.broadcasted_iota(jnp.int32, scores.shape, 0)
    col = lax.broadcasted_iota(jnp.int32, scores.shape, 1) + r * HEAD_DIM
    scores = jnp.where(row <= col, scores, -jnp.inf)
    weights = jnp.exp((scores - jnp.max(scores, axis=0, keepdims=True)) * SCALE)
    return weights * (1.0 / jnp.sum(weights, axis=0, keepdims=True))


def attend(qkv, h, block, context):
    cols = at(h, HEAD_DIM)
    r, mine, seen = block
    probs = probs_of_block(qkv, cols, r, mine, seen).astype(BF)
    context_t = lax.dot_general(qkv[2, seen, cols], probs, TN, preferred_element_type=F32)
    context[mine, cols] = context_t.T.astype(BF)


def attend_t(qkv, h, context_t, probs_t, x):
    cols = at(h, HEAD_DIM)
    for r, mine, seen in causal_blocks():
        probs = probs_of_block(qkv, cols, r, mine, seen)
        probs_t[h, seen, mine] = probs
        context_t[cols, at(x * (S // HEAD_DIM) + r, HEAD_DIM)] = lax.dot_general(
            qkv[2, seen, cols], probs.astype(BF), TN, preferred_element_type=F32
        ).astype(BF)


def attend_grad(qkv, h, probs_t, upstream, grads):
    cols = at(h, HEAD_DIM)
    dk, dv = [0.0] * 3, [0.0] * 3
    for r, mine, seen in causal_blocks():
        probs = probs_t[h, seen, mine]
        up = upstream[mine, cols]
        d_probs = lax.dot_general(qkv[2, seen, cols], up, NT, preferred_element_type=F32)
        total = jnp.sum(probs * d_probs, axis=0, keepdims=True)
        d_scores = (probs * (d_probs - total) * SCALE).astype(BF)
        dq_t = lax.dot_general(qkv[1, seen, cols], d_scores, TN, preferred_element_type=F32)
        grads[0, mine, cols] = dq_t.T.astype(BF)
        dk_r = jnp.dot(d_scores, qkv[0, mine, cols], preferred_element_type=F32)
        dv_r = jnp.dot(probs.astype(BF), up, preferred_element_type=F32)
        for j in range(r + 1):
            rows = slice(j * HEAD_DIM, (j + 1) * HEAD_DIM)
            dk[j] += dk_r[rows]
            dv[j] += dv_r[rows]
    for j in range(3):
        rows = pl.ds(j * HEAD_DIM, HEAD_DIM)
        grads[1, rows, cols] = dk[j].astype(BF)
        grads[2, rows, cols] = dv[j].astype(BF)


class Ring:
    def __init__(self, remote, me, plus, minus):
        self.remote, self.me, self.plus, self.minus = remote, me, plus, minus

    def gather_first(self, block, h, source=None):
        dst = block(self.me, h)
        copy = self.remote(dst if source is None else source, dst, (self.plus, self.minus)[h])
        copy.start()
        if h == 0:
            self.plus0 = copy
        else:
            self.minus1 = copy

    def gather_second(self, block, h, source=None):
        dst = block(self.me, h)
        copy = self.remote(dst if source is None else source, dst, (self.minus, self.plus)[h])
        copy.start()
        if h == 0:
            self.minus0 = copy
        else:
            self.plus1 = copy

    def gather_forward(self, block):
        prev, nxt = mod4(self.me - 1), mod4(self.me + 1)
        self.plus0.wait_recv()
        self.far0 = self.remote(block(prev, 0), block(prev, 0), self.plus)
        self.far0.start()
        self.minus1.wait_recv()
        self.far1 = self.remote(block(nxt, 1), block(nxt, 1), self.minus)
        self.far1.start()

    def gather_near(self):
        self.plus1.wait_recv()
        self.minus0.wait_recv()

    def gather_far(self):
        self.far0.wait_recv()
        self.far1.wait_recv()

    def reduce_far(self, part, got_far):
        far = mod4(self.me + 2)
        self.r0 = self.remote(part(far, 0), got_far.at[0], self.plus)
        self.r1 = self.remote(part(far, 1), got_far.at[1], self.minus)
        self.r0.start()
        self.r1.start()

    def reduce_near(self, part, got_near):
        nxt, prev = mod4(self.me + 1), mod4(self.me - 1)
        self.r2 = self.remote(part(nxt, 1), got_near.at[0, 1], self.plus)
        self.r3 = self.remote(part(prev, 0), got_near.at[1, 0], self.minus)
        self.r2.start()
        self.r3.start()

    def reduce_pass(self, part, got_far, got_near):
        nxt, prev = mod4(self.me + 1), mod4(self.me - 1)
        self.r0.wait_recv()
        ref = part(nxt, 0)
        ref[...] = (ref[...].astype(F32) + got_far[0].astype(F32)).astype(BF)
        self.r4 = self.remote(ref, got_near.at[0, 0], self.plus)
        self.r4.start()
        self.r1.wait_recv()
        ref = part(prev, 1)
        ref[...] = (ref[...].astype(F32) + got_far[1].astype(F32)).astype(BF)
        self.r5 = self.remote(ref, got_near.at[1, 1], self.minus)
        self.r5.start()

    def reduce_sum(self, part, got_near, h):
        for copy in ((self.r4, self.r3), (self.r2, self.r5))[h]:
            copy.wait_recv()
        total = part(self.me, h)[...].astype(F32)
        return total + got_near[0, h].astype(F32) + got_near[1, h].astype(F32)


def kernel(
    qkv_a_hbm, qkv_b_hbm, cot_hbm, w_hbm,
    out_ref, grads_ref, w_grad_ref,
    qkv_a, qkv_b, w_all, cot_all, cot_relay, ctx_a, ctx_a_all, ctx_b_all, probs_t,
    w_part, w_far, w_near, c_part, c_far, c_near, c_grad,
    o_own, o_other, o_got, o_far, o_near, o_done,
    send_sems, recv_sems, local_sems,
):
    dp, pipe, tensor = lax.axis_index("dp"), lax.axis_index("pipe"), lax.axis_index("tensor")
    x, z, y, core = dp // 4, lax.rem(dp, 4), tensor // 2, lax.rem(tensor, 2)

    def device(x=x, z=z, pipe=pipe, y=y, core=core):
        return (x * 4 + z, pipe, y * 2 + core)

    x_plus, x_minus = device(x=mod4(x + 1)), device(x=mod4(x - 1))
    y_plus, y_minus = device(y=mod4(y + 1)), device(y=mod4(y - 1))
    z_plus, z_minus = device(z=mod4(z + 1)), device(z=mod4(z - 1))
    twin, other_pipe = device(core=1 - core), device(pipe=1 - pipe)

    there = mod4(y - x + 2 * core)
    down, across = device(y=mod4(x + y + 2 * core)), device(x=there)
    home, away = device(x=there, y=x), device(x=y, y=mod4(x + y + 2 * core))
    stays_down, stays_across = lax.rem(x + 2 * core, 4) == 0, there == x
    stays_home = jnp.logical_and(there == x, y == x)

    barrier = pltpu.get_barrier_semaphore()
    for partner in (
        x_plus, x_minus, device(x=mod4(x + 2)), y_plus, y_minus, device(y=mod4(y + 2)),
        z_plus, z_minus, twin, other_pipe,
    ):
        pl.semaphore_signal(barrier, inc=1, device_id=partner, device_id_type=MESH)

    @pl.when(jnp.logical_not(stays_home))
    def _():
        for partner in (home, away):
            pl.semaphore_signal(barrier, inc=1, device_id=partner, device_id_type=MESH)

    pl.semaphore_wait(barrier, jnp.where(stays_home, 10, 12))

    made = []

    def remote(src, dst, where):
        copy = pltpu.make_async_remote_copy(
            src_ref=src, dst_ref=dst,
            send_sem=send_sems.at[len(made)], recv_sem=recv_sems.at[len(made)],
            device_id=where, device_id_type=MESH,
        )
        made.append(copy)
        return copy

    class Move:
        def __init__(self, src, dst_there, dst_here, where, stays, local_sem):
            self.stays, self.copy = stays, remote(src, dst_there, where)
            self.local = pltpu.make_async_copy(src, dst_here, local_sem)

        def start(self):
            pl.when(self.stays)(lambda: self.local.start())
            pl.when(jnp.logical_not(self.stays))(lambda: self.copy.start())

        def wait_recv(self):
            pl.when(self.stays)(lambda: self.local.wait())
            pl.when(jnp.logical_not(self.stays))(lambda: self.copy.wait_recv())

        def wait_send(self):
            pl.when(jnp.logical_not(self.stays))(lambda: self.copy.wait_send())

    moves = []

    def move(*args):
        moves.append(Move(*args))
        moves[-1].start()
        return moves[-1]

    def place_tokens(i):
        return mod4(i - x + 2 * core)

    def w_block(i, h):
        return w_all.at[pl.ds(h * S, S), at(i, S)]

    def cot_block(i, h):
        return cot_all.at[at(2 * place_tokens(i) + h, S // 2), at(core, W)]

    def a_rows(p, i):
        return at(p * 4 + i, HEAD_DIM)

    def ctx_a_block(p):
        return lambda i, h: ctx_a_all.at[a_rows(p, i), pl.ds(h * S, S)]

    def ctx_b_block(i, h):
        return ctx_b_all.at[pl.ds(h * S, S), at(i, S)]

    def w_part_block(i, h):
        return w_part.at[i, h]

    def c_part_block(i, h):
        return c_part.at[i, h]

    def o_block(p):
        return lambda i, h: o_own.at[a_rows(p, place_tokens(i)), pl.ds(h * S, S)]

    ring_w = Ring(remote, z, z_plus, z_minus)
    ring_cot = Ring(remote, y, y_plus, y_minus)
    ring_a = [Ring(remote, x, x_plus, x_minus) for _ in range(PIECES)]
    ring_b = Ring(remote, x, x_plus, x_minus)
    ring_wg = Ring(remote, z, z_plus, z_minus)
    ring_cg = Ring(remote, x, x_plus, x_minus)
    ring_out = [Ring(remote, y, y_plus, y_minus) for _ in range(PIECES)]

    for h in (0, 1):
        ring_w.gather_first(w_block, h, w_hbm.at[pl.ds(h * S, S)])
    downs = []
    for h in (0, 1):
        half = pl.ds(h * (S // 2), S // 2)
        downs.append(
            move(cot_hbm.at[half], cot_relay.at[h], cot_relay.at[h], down, stays_down, local_sems.at[h])
        )

    load_a = pltpu.make_async_copy(qkv_a_hbm, qkv_a, local_sems.at[2])
    load_b = pltpu.make_async_copy(qkv_b_hbm, qkv_b, local_sems.at[3])
    load_w = pltpu.make_async_copy(w_hbm, w_all.at[:, at(z, S)], local_sems.at[4])
    load_a.start()
    load_b.start()
    load_w.start()

    handed = []
    load_a.wait()
    for block in causal_blocks():
        def head_a(h, carry, block=block):
            attend(qkv_a, h, block, ctx_a)
            return carry
        lax.fori_loop(0, HEADS, head_a, 0, unroll=3)
        p = block[0]
        copy = remote(ctx_a.at[block[1]], ctx_a_all.at[a_rows(p, x)], other_pipe)
        copy.start()
        handed.append(copy)

    acrosses = []
    for h in (0, 1):
        downs[h].wait_recv()
        landing = cot_all.at[at(2 * x + h, S // 2), at(core, W)]
        acrosses.append(
            move(cot_relay.at[h], landing, landing, across, stays_across, local_sems.at[5 + h])
        )

    load_b.wait()
    for h in (0, 1):
        def head_b(i, carry, h=h):
            attend_t(qkv_b, h * (HEADS // 2) + i, ctx_b_all, probs_t, x)
            return carry
        lax.fori_loop(0, HEADS // 2, head_b, 0, unroll=True)
        ring_b.gather_first(ctx_b_block, h)
        ring_b.gather_second(ctx_b_block, h)

    def to_twin(ref):
        copy = remote(ref, ref, twin)
        copy.start()
        return copy

    twins = []
    for h in (0, 1):
        acrosses[h].wait_recv()
        ring_cot.gather_first(cot_block, h)
        ring_cot.gather_second(cot_block, h)
        twins.append(to_twin(cot_block(y, h)))
    ring_w.gather_forward(w_block)
    for h in (0, 1):
        ring_w.gather_second(w_block, h, w_hbm.at[pl.ds(h * S, S)])
    ring_b.gather_forward(ctx_b_block)
    for p in range(PIECES):
        handed[p].wait_recv()
        for h in (0, 1):
            ring_a[p].gather_first(ctx_a_block(p), h)
        for h in (0, 1):
            ring_a[p].gather_second(ctx_a_block(p), h)
    ring_cot.gather_forward(cot_block)
    ring_cot.gather_near()
    for i in (mod4(y - 1), mod4(y + 1)):
        twins.append(to_twin(cot_all.at[at(place_tokens(i), S), at(core, W)]))
    ring_b.gather_near()
    ring_b.gather_far()
    for p in range(PIECES):
        ring_a[p].gather_forward(ctx_a_block(p))
    ring_cot.gather_far()
    twins.append(to_twin(cot_all.at[at(place_tokens(y + 2), S), at(core, W)]))
    for copy in twins:
        copy.wait_recv()

    def w_term(i):
        def rows(r, carry):
            w_part[i, r] = jnp.dot(
                ctx_b_all[at(r, S), :], cot_all[:, at(i, S)], preferred_element_type=F32
            ).astype(BF)
            return carry
        lax.fori_loop(0, 2, rows, 0)

    w_term(mod4(z + 2))
    ring_wg.reduce_far(w_part_block, w_far)
    w_term(mod4(z + 1))
    w_term(mod4(z - 1))
    ring_wg.reduce_near(w_part_block, w_near)
    w_term(z)

    load_w.wait()
    ring_w.gather_near()
    ring_w.gather_far()

    def o_term(p, side):
        return jnp.dot(
            ctx_a_all[at(p, 4 * HEAD_DIM), :], w_all[:, at(side, W)], preferred_element_type=F32
        )

    swaps = []
    for p in range(PIECES):
        ring_a[p].gather_near()
        ring_a[p].gather_far()
        rows = at(p, 4 * HEAD_DIM)
        o_other[rows] = o_term(p, 1 - core).astype(BF)
        copy = remote(o_other.at[rows], o_got.at[rows], twin)
        copy.start()
        swaps.append(copy)

    for p in range(PIECES):
        rows = at(p, 4 * HEAD_DIM)
        term = o_term(p, core)
        swaps[p].wait_recv()
        o_own[rows] = (term + o_got[rows].astype(F32)).astype(BF)
        ring_out[p].reduce_far(o_block(p), o_far.at[p])
        ring_out[p].reduce_near(o_block(p), o_near.at[p])
        if p > 0:
            ring_out[p - 1].reduce_pass(o_block(p - 1), o_far.at[p - 1], o_near.at[p - 1])

    def c_term(i):
        def rows(r, carry):
            c_part[i, r] = lax.dot_general(
                cot_all[at(2 * i + r, S // 2), :], w_all[...], NT, preferred_element_type=F32
            ).astype(BF)
            return carry
        lax.fori_loop(0, 2, rows, 0)

    back = []

    def o_finish(p):
        rows = pl.ds(p * HEAD_DIM, HEAD_DIM)
        for h in (0, 1):
            o_done[rows, pl.ds(h * S, S)] = (
                ring_out[p].reduce_sum(o_block(p), o_near.at[p], h).astype(BF)
            )
        back.append(
            move(
                o_done.at[rows], out_ref.at[rows], out_ref.at[rows], home, stays_home, local_sems.at[7 + p]
            )
        )

    c_term(mod4(x + 2))
    ring_cg.reduce_far(c_part_block, c_far)
    ring_out[2].reduce_pass(o_block(2), o_far.at[2], o_near.at[2])
    c_term(mod4(x + 1))
    c_term(mod4(x - 1))
    ring_cg.reduce_near(c_part_block, c_near)
    c_term(x)
    ring_wg.reduce_pass(w_part_block, w_far, w_near)
    ring_cg.reduce_pass(c_part_block, c_far, c_near)
    o_finish(0)
    o_finish(1)
    o_finish(2)

    for h in (0, 1):
        c_grad[pl.ds(h * (S // 2), S // 2)] = ring_cg.reduce_sum(c_part_block, c_near, h).astype(BF)

    def head_grad(h, carry):
        attend_grad(qkv_b, h, probs_t, c_grad, grads_ref)
        return carry

    lax.fori_loop(0, HEADS, head_grad, 0, unroll=2)

    for h in (0, 1):
        w_grad_ref[pl.ds(h * S, S)] = (
            ring_wg.reduce_sum(w_part_block, w_near, h) / lax.axis_size("dp")
        ).astype(BF)

    for copy in back:
        copy.wait_recv()

    moved = [m.copy for m in moves]
    for copy in made:
        if not any(copy is other for other in moved):
            copy.wait_send()
    for m in moves:
        m.wait_send()


def body(sent_qkv, saved_qkv, cotangent, out_weight):
    bf = lambda *shape: pltpu.VMEM(shape, BF)
    half = S // 2
    out, grads, w_grad = pl.pallas_call(
        kernel,
        out_shape=(
            jax.ShapeDtypeStruct((S, W), BF),
            jax.ShapeDtypeStruct((3, S, W), BF),
            jax.ShapeDtypeStruct((W, S), BF),
        ),
        in_specs=[pl.BlockSpec(memory_space=pl.ANY)] * 4,
        out_specs=(pl.BlockSpec(memory_space=pltpu.VMEM),) * 3,
        scratch_shapes=[
            bf(3, S, W), bf(3, S, W),
            bf(W, 4 * S), bf(4 * S, 2 * W), bf(2, half, W),
            bf(S, W), bf(4 * S, W), bf(W, 4 * S),
            pltpu.VMEM((HEADS, S, S), F32),
            bf(4, 2, S, S), bf(2, S, S), bf(2, 2, S, S),
            bf(4, 2, half, W), bf(2, half, W), bf(2, 2, half, W), bf(S, W),
            bf(4 * S, W), bf(4 * S, W), bf(4 * S, W),
            bf(PIECES, 2, HEAD_DIM, S), bf(PIECES, 2, 2, HEAD_DIM, S), bf(S, W),
            pltpu.SemaphoreType.DMA((N_SEMS,)),
            pltpu.SemaphoreType.DMA((N_SEMS,)),
            pltpu.SemaphoreType.DMA((10,)),
        ],
        compiler_params=pltpu.CompilerParams(
            collective_id=0, has_side_effects=True, vmem_limit_bytes=56 << 20
        ),
        cost_estimate=pl.CostEstimate(
            flops=13_000_000_000, bytes_accessed=16_000_000, transcendentals=1_800_000
        ),
    )(
        jnp.transpose(sent_qkv[0, 0], (1, 0, 2)),
        jnp.transpose(saved_qkv[0, 0], (1, 0, 2)),
        cotangent[0, 0],
        out_weight[0],
    )
    return out[None, None], jnp.transpose(grads, (1, 0, 2))[None, None], w_grad[None]


def solution(mesh):
    in_specs = (
        P("pipe", "dp", None, None, "tensor"),
        P("pipe", "dp", None, None, "tensor"),
        P("pipe", "dp", None, "tensor"),
        P("pipe", "tensor", "dp"),
    )
    out_specs = (
        P("pipe", "dp", None, "tensor"),
        P("pipe", "dp", None, None, "tensor"),
        P("pipe", "tensor", "dp"),
    )
    return jax.shard_map(body, mesh=mesh, in_specs=in_specs, out_specs=out_specs, check_vma=False)
```

time: 157 us -> 121 us (0.77)
  the two profiles are of different devices: /device:TPU:156 before, /device:TPU:38 now
where the time goes in v2:
time: 121 us
  Pallas kernels  115 us (95%)
  local copies, waits for them, and re-layouts  5.59 us (5%)
    pallas_call x1, Pallas kernels, body(): pl.pallas_call(kernel, out_shape=(jax.ShapeDtypeStruct((S, W), BF), jax.S...  115 us
    unnamed x5, local copies, waits for them, and re-layouts  5.59 us

profile of v2, /device:TPU:38, one launch (start us, length us, event | category | flops | bytes accessed | tf_op | source)
XLA Modules:
  0.0 121.3 jit_solution(15689041299358595946)
XLA Ops:
  0.6 115.0 %shard_map.67 = (bf16[384,768]{1,0:T(8,128)(2,1)}, bf16[3,384,768]{2,1,0:T(8,128)(2,1)}, bf16[768,384]{1,0:T(8,128)(2,1)}) custom-call(bf16[3,384,768]{2,1,0:T(8,128)(2,1)} %bitcast.16, bf16[3,384,768]{2,1,0:T(8,128)(2,1)} %bitcast.17, bf16[384,768]{1,0:T(8,128)(2,1)} %bitcast.18, bf16[768,384]{1,0:T(8,128)(2,1)} %bitcast.19), custom_call_target="tpu_custom_call" | custom-call | flops 12999999488 | bytes 16000000 | tf_op jit(solution)/shard_map/pallas_call | solution.py:455
  115.7 1.9 %copy.10 = bf16[1,1,384,768]{3,2,1,0:T(8,128)(2,1)} copy(bf16[1,1,384,768]{3,2,1,0:T(8,128)(2,1)} %bitcast.15) | data formatting | bytes 1179648
  117.6 0.0 copy-start
  117.6 2.9 %copy.11 = bf16[1,1,384,3,768]{4,2,3,1,0:T(8,128)(2,1)} copy(bf16[1,1,384,3,768]{4,2,3,1,0:T(8,128)(2,1)} %bitcast.13) | data formatting | bytes 3538944
  120.5 0.0 copy-done
  120.5 0.8 copy.12
Async XLA Ops:
  117.6 2.9 %copy-start = (bf16[768,384]{1,0:T(8,128)(2,1)S(1)}, bf16[768,384]{1,0:T(8,128)(2,1)}, u32[]{:S(2)}) copy-start(bf16[768,384]{1,0:T(8,128)(2,1)} %get-tuple-element.8) | copy-start | bytes 1769476

commit v3 on v2

--- a/solution.py
+++ b/solution.py
@@ -345,20 +345,19 @@
     for copy in twins:
         copy.wait_recv()
 
-    def w_term(i):
+    def w_terms(pair):
         def rows(r, carry):
-            w_part[i, r] = jnp.dot(
-                ctx_b_all[at(r, S), :], cot_all[:, at(i, S)], preferred_element_type=F32
+            term = jnp.dot(
+                ctx_b_all[at(r, S), :], cot_all[:, at(pair, W)], preferred_element_type=F32
             ).astype(BF)
+            w_part[2 * pair, r], w_part[2 * pair + 1, r] = term[:, :S], term[:, S:]
             return carry
         lax.fori_loop(0, 2, rows, 0)
 
-    w_term(mod4(z + 2))
+    w_terms(1 - z // 2)
     ring_wg.reduce_far(w_part_block, w_far)
-    w_term(mod4(z + 1))
-    w_term(mod4(z - 1))
+    w_terms(z // 2)
     ring_wg.reduce_near(w_part_block, w_near)
-    w_term(z)
 
     load_w.wait()
     ring_w.gather_near()
@@ -369,33 +368,11 @@
             ctx_a_all[at(p, 4 * HEAD_DIM), :], w_all[:, at(side, W)], preferred_element_type=F32
         )
 
-    swaps = []
-    for p in range(PIECES):
-        ring_a[p].gather_near()
-        ring_a[p].gather_far()
-        rows = at(p, 4 * HEAD_DIM)
-        o_other[rows] = o_term(p, 1 - core).astype(BF)
-        copy = remote(o_other.at[rows], o_got.at[rows], twin)
-        copy.start()
-        swaps.append(copy)
-
-    for p in range(PIECES):
-        rows = at(p, 4 * HEAD_DIM)
-        term = o_term(p, core)
-        swaps[p].wait_recv()
-        o_own[rows] = (term + o_got[rows].astype(F32)).astype(BF)
-        ring_out[p].reduce_far(o_block(p), o_far.at[p])
-        ring_out[p].reduce_near(o_block(p), o_near.at[p])
-        if p > 0:
-            ring_out[p - 1].reduce_pass(o_block(p - 1), o_far.at[p - 1], o_near.at[p - 1])
-
     def c_term(i):
-        def rows(r, carry):
-            c_part[i, r] = lax.dot_general(
-                cot_all[at(2 * i + r, S // 2), :], w_all[...], NT, preferred_element_type=F32
-            ).astype(BF)
-            return carry
-        lax.fori_loop(0, 2, rows, 0)
+        term = lax.dot_general(
+            cot_all[at(i, S), :], w_all[...], NT, preferred_element_type=F32
+        ).astype(BF)
+        c_part[i, 0], c_part[i, 1] = term[: S // 2], term[S // 2 :]
 
     back = []
 
@@ -413,13 +390,32 @@
 
     c_term(mod4(x + 2))
     ring_cg.reduce_far(c_part_block, c_far)
-    ring_out[2].reduce_pass(o_block(2), o_far.at[2], o_near.at[2])
+    swaps = []
+    for p in range(PIECES):
+        ring_a[p].gather_near()
+        ring_a[p].gather_far()
+        rows = at(p, 4 * HEAD_DIM)
+        o_other[rows] = o_term(p, 1 - core).astype(BF)
+        copy = remote(o_other.at[rows], o_got.at[rows], twin)
+        copy.start()
+        swaps.append(copy)
+
+    for p in range(PIECES):
+        rows = at(p, 4 * HEAD_DIM)
+        term = o_term(p, core)
+        swaps[p].wait_recv()
+        o_own[rows] = (term + o_got[rows].astype(F32)).astype(BF)
+        ring_out[p].reduce_far(o_block(p), o_far.at[p])
+        ring_out[p].reduce_near(o_block(p), o_near.at[p])
+
     c_term(mod4(x + 1))
     c_term(mod4(x - 1))
     ring_cg.reduce_near(c_part_block, c_near)
+    for p in range(PIECES):
+        ring_out[p].reduce_pass(o_block(p), o_far.at[p], o_near.at[p])
     c_term(x)
+    ring_cg.reduce_pass(c_part_block, c_far, c_near)
     ring_wg.reduce_pass(w_part_block, w_far, w_near)
-    ring_cg.reduce_pass(c_part_block, c_far, c_near)
     o_finish(0)
     o_finish(1)
     o_finish(2)

time: 121 us -> 113 us (0.934)
  the two profiles are of different devices: /device:TPU:38 before, /device:TPU:1 now
where the time goes in v3:
time: 113 us
  Pallas kernels  106 us (94%)
  local copies, waits for them, and re-layouts  5.59 us (5%)
    pallas_call x1, Pallas kernels, body(): pl.pallas_call(kernel, out_shape=(jax.ShapeDtypeStruct((S, W), BF), jax.S...  106 us
    unnamed x5, local copies, waits for them, and re-layouts  5.59 us

profile of v3, /device:TPU:1, one launch (start us, length us, event | category | flops | bytes accessed | tf_op | source)
XLA Modules:
  0.0 112.7 jit_solution(1038628438535527067)
XLA Ops:
  0.6 106.5 %shard_map.67 = (bf16[384,768]{1,0:T(8,128)(2,1)}, bf16[3,384,768]{2,1,0:T(8,128)(2,1)}, bf16[768,384]{1,0:T(8,128)(2,1)}) custom-call(bf16[3,384,768]{2,1,0:T(8,128)(2,1)} %bitcast.16, bf16[3,384,768]{2,1,0:T(8,128)(2,1)} %bitcast.17, bf16[384,768]{1,0:T(8,128)(2,1)} %bitcast.18, bf16[768,384]{1,0:T(8,128)(2,1)} %bitcast.19), custom_call_target="tpu_custom_call" | custom-call | flops 12999999488 | bytes 16000000 | tf_op jit(solution)/shard_map/pallas_call | solution.py:451
  107.1 1.9 %copy.10 = bf16[1,1,384,768]{3,2,1,0:T(8,128)(2,1)} copy(bf16[1,1,384,768]{3,2,1,0:T(8,128)(2,1)} %bitcast.15) | data formatting | bytes 1179648
  109.0 0.0 copy-start
  109.0 2.9 %copy.11 = bf16[1,1,384,3,768]{4,2,3,1,0:T(8,128)(2,1)} copy(bf16[1,1,384,3,768]{4,2,3,1,0:T(8,128)(2,1)} %bitcast.13) | data formatting | bytes 3538944
  111.9 0.0 copy-done
  111.9 0.8 copy.12
Async XLA Ops:
  109.0 2.9 %copy-start = (bf16[768,384]{1,0:T(8,128)(2,1)S(1)}, bf16[768,384]{1,0:T(8,128)(2,1)}, u32[]{:S(2)}) copy-start(bf16[768,384]{1,0:T(8,128)(2,1)} %get-tuple-element.8) | copy-start | bytes 1769476

commit v4 on v3

--- a/solution.py
+++ b/solution.py
@@ -163,7 +163,7 @@
     out_ref, grads_ref, w_grad_ref,
     qkv_a, qkv_b, w_all, cot_all, cot_relay, ctx_a, ctx_a_all, ctx_b_all, probs_t,
     w_part, w_far, w_near, c_part, c_far, c_near, c_grad,
-    o_own, o_other, o_got, o_far, o_near, o_done,
+    o_own, o_other, o_got, o_far, o_near, o_done, grads_v, w_grad_v,
     send_sems, recv_sems, local_sems,
 ):
     dp, pipe, tensor = lax.axis_index("dp"), lax.axis_index("pipe"), lax.axis_index("tensor")
@@ -424,18 +424,27 @@
         c_grad[pl.ds(h * (S // 2), S // 2)] = ring_cg.reduce_sum(c_part_block, c_near, h).astype(BF)
 
     def head_grad(h, carry):
-        attend_grad(qkv_b, h, probs_t, c_grad, grads_ref)
+        attend_grad(qkv_b, h, probs_t, c_grad, grads_v)
         return carry
 
     lax.fori_loop(0, HEADS, head_grad, 0, unroll=2)
-
-    for h in (0, 1):
-        w_grad_ref[pl.ds(h * S, S)] = (
+    stores = [pltpu.make_async_copy(grads_v, grads_ref, local_sems.at[10])]
+    stores[0].start()
+
+    for h in (0, 1):
+        rows = pl.ds(h * S, S)
+        w_grad_v[rows] = (
             ring_wg.reduce_sum(w_part_block, w_near, h) / lax.axis_size("dp")
         ).astype(BF)
+        stores.append(
+            pltpu.make_async_copy(w_grad_v.at[rows], w_grad_ref.at[rows], local_sems.at[11 + h])
+        )
+        stores[-1].start()
 
     for copy in back:
         copy.wait_recv()
+    for copy in stores:
+        copy.wait()
 
     moved = [m.copy for m in moves]
     for copy in made:
@@ -456,7 +465,7 @@
             jax.ShapeDtypeStruct((W, S), BF),
         ),
         in_specs=[pl.BlockSpec(memory_space=pl.ANY)] * 4,
-        out_specs=(pl.BlockSpec(memory_space=pltpu.VMEM),) * 3,
+        out_specs=(pl.BlockSpec(memory_space=pl.ANY),) * 3,
         scratch_shapes=[
             bf(3, S, W), bf(3, S, W),
             bf(W, 4 * S), bf(4 * S, 2 * W), bf(2, half, W),
@@ -466,9 +475,10 @@
             bf(4, 2, half, W), bf(2, half, W), bf(2, 2, half, W), bf(S, W),
             bf(4 * S, W), bf(4 * S, W), bf(4 * S, W),
             bf(PIECES, 2, HEAD_DIM, S), bf(PIECES, 2, 2, HEAD_DIM, S), bf(S, W),
+            bf(3, S, W), bf(W, S),
             pltpu.SemaphoreType.DMA((N_SEMS,)),
             pltpu.SemaphoreType.DMA((N_SEMS,)),
-            pltpu.SemaphoreType.DMA((10,)),
+            pltpu.SemaphoreType.DMA((13,)),
         ],
         compiler_params=pltpu.CompilerParams(
             collective_id=0, has_side_effects=True, vmem_limit_bytes=56 << 20

time: 113 us -> 112 us (level)
  no operation moved by 1% of the time
where the time goes in v4:
time: 112 us
  Pallas kernels  106 us (95%)
  local copies, waits for them, and re-layouts  5.59 us (5%)
    pallas_call x1, Pallas kernels, body(): pl.pallas_call(kernel, out_shape=(jax.ShapeDtypeStruct((S, W), BF), jax.S...  106 us
    unnamed x5, local copies, waits for them, and re-layouts  5.59 us

profile of v4, /device:TPU:1, one launch (start us, length us, event | category | flops | bytes accessed | tf_op | source)
XLA Modules:
  0.0 111.9 jit_solution(624810823287047768)
XLA Ops:
  0.6 105.6 %shard_map.67 = (bf16[384,768]{1,0:T(8,128)(2,1)}, bf16[3,384,768]{2,1,0:T(8,128)(2,1)}, bf16[768,384]{1,0:T(8,128)(2,1)}) custom-call(bf16[3,384,768]{2,1,0:T(8,128)(2,1)} %bitcast.16, bf16[3,384,768]{2,1,0:T(8,128)(2,1)} %bitcast.17, bf16[384,768]{1,0:T(8,128)(2,1)} %bitcast.18, bf16[768,384]{1,0:T(8,128)(2,1)} %bitcast.19), custom_call_target="tpu_custom_call" | custom-call | flops 12999999488 | bytes 16000000 | tf_op jit(solution)/shard_map/pallas_call | solution.py:460
  106.3 1.9 %copy.10 = bf16[1,1,384,768]{3,2,1,0:T(8,128)(2,1)} copy(bf16[1,1,384,768]{3,2,1,0:T(8,128)(2,1)} %bitcast.15) | data formatting | bytes 1179648
  108.2 0.0 copy-start
  108.2 2.9 %copy.11 = bf16[1,1,384,3,768]{4,2,3,1,0:T(8,128)(2,1)} copy(bf16[1,1,384,3,768]{4,2,3,1,0:T(8,128)(2,1)} %bitcast.13) | data formatting | bytes 3538944
  111.1 0.0 copy-done
  111.1 0.8 copy.12
Async XLA Ops:
  108.2 2.9 %copy-start = (bf16[768,384]{1,0:T(8,128)(2,1)S(1)}, bf16[768,384]{1,0:T(8,128)(2,1)}, u32[]{:S(2)}) copy-start(bf16[768,384]{1,0:T(8,128)(2,1)} %get-tuple-element.8) | copy-start | bytes 1769476
